TPU v7x, 768 devices: a whole 4x8x12 slice. The times are simulated.
768 devices in a mesh: replica: 64 (over y, z_lo, core), fsdp: 12 (over x, z_hi).
Axes of the slice: x: 4, y: 8, z: 12 (z_hi: 3, z_lo: 4; z = z_hi * 4 + z_lo), core: 2. Of those that a mesh axis runs over, the one named last changes fastest.
Arguments:
- tokens: bfloat16 [64, 2688, 4608], P('replica', 'fsdp'), may hold values from -6 to 6
- key_weight: bfloat16 [64, 4608, 512], P('replica', 'fsdp'), may hold values from -0.09375 to 0.09375
- deltas: bfloat16 [64, 192, 28672], P('replica', 'fsdp'), may hold values from -16 to 16
- params: float32 [192, 28672], P('fsdp', 'replica'), may hold values from -6 to 6
- momentum: float32 [192, 28672], P('fsdp', 'replica'), may hold values from -3 to 3
Outputs:
- new_params: float32 [192, 28672], P('fsdp', 'replica')
- new_momentum: float32 [192, 28672], P('fsdp', 'replica')
- merged_weights: bfloat16 [192, 28672], P('fsdp')
- keys: bfloat16 [64, 2688, 512], P('replica', 'fsdp')
All inputs are finite; a program needn't handle non-finite values.
Results may differ from a plain program's by a relative error of at most 0.001.
Values may be sent and summed in bfloat16 or wider, within the bound.
No kernel may reach another device: no remote copies, remote signals or barrier semaphores. Data moves between devices by JAX's collectives and lax.ppermute only.
A program may use at most 128 MiB of HBM per device.

v0:
```python
import jax
import jax.numpy as jnp
from jax import lax
from jax.sharding import PartitionSpec as P

outer_rate = 0.7
outer_decay = 0.9


def inner_keys(activation, weight_local):
    summed = jnp.dot(
        activation,
        lax.all_gather(weight_local, "fsdp", axis=0, tiled=True),
        preferred_element_type=jnp.float32,
    )
    return summed.astype(jnp.bfloat16)[None]


def outer_update(delta_block, params, momentum):
    replicas = lax.axis_size("replica")
    summed = lax.psum_scatter(
        delta_block[0].astype(jnp.float32), "replica", scatter_dimension=1, tiled=True
    )
    outer_grad = summed / replicas
    new_momentum = outer_decay * momentum + outer_grad
    new_params = params - outer_rate * (outer_grad + outer_decay * new_momentum)
    merged_weights = lax.all_gather(new_params.astype(jnp.bfloat16), "replica", axis=1, tiled=True)
    return (new_params, new_momentum, merged_weights)


def local(tokens, key_weight, deltas, params, momentum):
    keys = inner_keys(tokens[0], key_weight[0])
    new_params, new_momentum, merged_weights = outer_update(deltas, params, momentum)
    return (new_params, new_momentum, merged_weights, keys)


def solution(mesh):
    return jax.shard_map(
        local,
        mesh=mesh,
        in_specs=(
            P("replica", "fsdp", None),
            P("replica", "fsdp", None),
            P("replica", "fsdp", None),
            P("fsdp", "replica"),
            P("fsdp", "replica"),
        ),
        out_specs=(
            P("fsdp", "replica"),
            P("fsdp", "replica"),
            P("fsdp", None),
            P("replica", "fsdp", None),
        ),
        check_vma=False,
    )
```

profile of v0, /device:TPU:1, one launch (start us, length us, event | category | flops | bytes accessed | tf_op | source)
XLA Modules:
  0.0 504.3 jit_solution(10314373106693937800)
XLA Ops:
  8.0 0.0 copy-start
  8.0 0.0 reduce-scatter.4.cloned.1.call-start
  8.1 2.7 bitcast_convert_fusion
  10.7 8.6 %copy.11 = f32[16,28672]{0,1:T(8,128)} copy(f32[16,28672]{1,0:T(8,128)} %bitcast_convert_fusion) | data formatting | bytes 3670016
  19.4 0.0 copy-start.1
  19.4 0.0 copy-start.2
  19.4 0.0 reduce-scatter.4.cloned.1.call-update
  19.4 0.0 all-gather.4.cloned.1.call-start
  19.5 0.5 all-gather.4.cloned.1.call-update
  20.0 386.7 %reduce-scatter.4.cloned.1.call-done = f32[448,16]{1,0:T(8,128)} async-done(((f32[28672,16]{1,0:T(8,128)}), f32[448,16]{1,0:T(8,128)}) %reduce-scatter.4.cloned.1.call-update) | async-done | bytes 28688
  406.7 1.0 copy.12
  407.8 0.0 copy-done.1
  407.8 0.0 copy-done.2
  407.8 0.6 convert_bitcast_fusion
  408.4 81.5 %all-gather.1 = bf16[64,448,16]{1,2,0:T(8,128)(2,1)S(1)} all-gather(bf16[1,448,16]{1,2,0:T(8,128)(2,1)S(1)} %get-tuple-element.4), channel_id=1, replica_groups=mesh['replica'=64,'fsdp'=12] {'replica'}, dimensions={0}, use_global_device_ids=true | all-gather | bytes 931840 | tf_op jit(solution)/shard_map/all_gather | solution.py:27
  489.9 0.6 copy.10
  490.4 2.1 reshape.13
  492.6 0.0 all-gather.4.cloned.1.call-done
  492.6 0.0 copy-done
  492.6 4.3 fusion.8
Async XLA Ops:
  8.0 484.6 %copy-start = (bf16[1,224,4608]{2,1,0:T(8,128)(2,1)S(1)}, bf16[1,224,4608]{2,1,0:T(8,128)(2,1)}, u32[]{:S(2)}) copy-start(bf16[1,224,4608]{2,1,0:T(8,128)(2,1)} %param.5) | copy-start | bytes 6193156
  8.0 398.7 %reduce-scatter.4.cloned.1.call-start = ((), (), s32[]{:S(2)}) async-start(), calls=%async_computation.2 | async-start | bytes 14909440
  19.4 388.4 %copy-start.1 = (f32[16,448]{1,0:T(8,128)S(1)}, f32[16,448]{1,0:T(8,128)}, u32[]{:S(2)}) copy-start(f32[16,448]{1,0:T(8,128)} %param.8) | copy-start | bytes 86020
  19.4 388.4 %copy-start.2 = (f32[16,448]{1,0:T(8,128)S(1)}, f32[16,448]{1,0:T(8,128)}, u32[]{:S(2)}) copy-start(f32[16,448]{1,0:T(8,128)} %param.9) | copy-start | bytes 86020
  19.4 473.1 %all-gather.4.cloned.1.call-start = ((), (), s32[]{:S(2)}) async-start(), calls=%async_computation.1 | async-start | bytes 5111808 | tf_op jit(solution)/shard_map/all_gather | solution.py:13
Sparse Core Ops, SparseCore 0:
  19.5 387.1 reduce-scatter.3
Sparse Core Ops, SparseCore 1:
  23.9 142.3 all-gather.3
where the time goes:
time: 508 us; the launch traced here: 504 us
  waiting for transfers between devices  387 us (76%)
  blocking collectives  81.5 us (16%)
  between operations  15.5 us (3%)
  local copies, waits for them, and re-layouts  12.4 us (2%)
    unnamed x3, waiting for transfers between devices  387 us
    all_gather x1, blocking collectives, outer_update(): lax.all_gather(new_params.astype(jnp.bfloat16), 'replica', axis=1, tiled=...  81.5 us
    unnamed x9, local copies, waits for them, and re-layouts  11.8 us
  transfers between devices with their start and end apart: 2, of which 1 were waited for; matrix products, arithmetic and copies ran while one was open for 1% of the time, Pallas kernels for 0%

commit v1 on v0

v1 whole, which is shorter than its diff:
```python
import functools

import jax
import jax.numpy as jnp
from jax import lax
from jax.experimental import pallas as pl
from jax.experimental.pallas import tpu as pltpu
from jax.sharding import PartitionSpec as P

outer_rate = 0.7
outer_decay = 0.9

X, ZH, Y, ZL = 4, 3, 8, 4
x_rings = [[x * ZH + z for x in range(X)] for z in range(ZH)]
z_rings = [[x * ZH + z for z in range(ZH)] for x in range(X)]
y_rings = [[(y * ZL + z) * 2 + c for y in range(Y)] for z in range(ZL) for c in range(2)]
z_lines = [[(y * ZL + z) * 2 + c for z in range(ZL)] for y in range(Y) for c in range(2)]
zc_groups = [[(y * ZL + z) * 2 + c for z in range(ZL) for c in range(2)] for y in range(Y)]
same_core = [[2 * i + c for i in range(32)] for c in range(2)]
cores = [(i, i ^ 1) for i in range(64)]


def z_shift(step):
    return [(x * ZH + z, x * ZH + (z + step) % ZH) for x in range(X) for z in range(ZH)]


def x_shift(step):
    return [(x * ZH + z, (x + step) % X * ZH + z) for x in range(X) for z in range(ZH)]


def spread(block, groups):
    copies = jnp.broadcast_to(block, (len(groups[0]),) + block.shape)
    return lax.all_to_all(copies, "replica", 0, 0, axis_index_groups=groups)


def matmul_kernel(block_ref, token_ref, start_ref, *refs):
    *weight_refs, out_ref = refs
    total = start_ref[...].astype(jnp.float32)
    index = 0
    for weight_ref in weight_refs:
        count, depth, _ = weight_ref.shape
        for part in range(count):
            columns = pl.ds(pl.multiple_of(block_ref[index] * depth, 128), depth)
            total += jnp.dot(
                token_ref[:, columns], weight_ref[part], preferred_element_type=jnp.float32
            )
            index += 1
    out_ref[...] = total.astype(out_ref.dtype)


def project(blocks, activation, weights, start, dtype):
    tokens, features = activation.shape
    width = weights[0].shape[-1]
    tile = width // 2
    out_spec = pl.BlockSpec((tokens, tile), lambda i, b: (0, i))
    depth = sum(w.shape[0] * w.shape[1] for w in weights)
    return pl.pallas_call(
        matmul_kernel,
        grid_spec=pltpu.PrefetchScalarGridSpec(
            num_scalar_prefetch=1,
            grid=(2,),
            in_specs=[pl.BlockSpec((tokens, features), lambda i, b: (0, 0)), out_spec]
            + [pl.BlockSpec(w.shape[:2] + (tile,), lambda i, b: (0, 0, i)) for w in weights],
            out_specs=out_spec,
        ),
        out_shape=jax.ShapeDtypeStruct((tokens, width), dtype),
        cost_estimate=pl.CostEstimate(
            flops=2 * depth * tokens * width,
            bytes_accessed=2 * depth * width + 2 * tokens * features + 6 * tokens * width,
            transcendentals=0,
        ),
        compiler_params=pltpu.CompilerParams(vmem_limit_bytes=32 * 2**20),
    )(blocks, activation, start, *weights)


def update(summed, params, momentum):
    outer_grad = summed / lax.axis_size("replica")
    new_momentum = outer_decay * momentum + outer_grad
    new_params = params - outer_rate * (outer_grad + outer_decay * new_momentum)
    return new_params, new_momentum


def assemble_kernel(core_ref, own_ref, other_ref, out_ref):
    zs, ys, _, width = own_ref.shape
    even = core_ref[0] == 0
    for y in range(ys):
        for z in range(zs):
            own, other = own_ref[z, y], other_ref[z, y]
            at = (y * zs + z) * 2 * width
            out_ref[:, at : at + 2 * width] = jnp.concatenate(
                [jnp.where(even, own, other), jnp.where(even, other, own)], axis=1
            )


def assemble(own):
    zs, ys, rows, width = own.shape
    other = lax.ppermute(own, "replica", cores)
    core = (lax.axis_index("replica") % 2).astype(jnp.int32)[None]
    part = pl.BlockSpec((zs, ys // 2, rows, width), lambda y, c: (0, y, 0, 0))
    return pl.pallas_call(
        assemble_kernel,
        grid_spec=pltpu.PrefetchScalarGridSpec(
            num_scalar_prefetch=1,
            grid=(2,),
            in_specs=[part, part],
            out_specs=pl.BlockSpec((rows, zs * ys * width), lambda y, c: (0, y)),
        ),
        out_shape=jax.ShapeDtypeStruct((rows, zs * ys * 2 * width), own.dtype),
    )(core, own, other)

def local(tokens, key_weight, deltas, params, momentum):
    activation, weight, delta = tokens[0], key_weight[0], deltas[0]
    x, z = lax.axis_index("fsdp") // ZH, lax.axis_index("fsdp") % ZH
    rows, columns = delta.shape

    from_below = lax.ppermute(weight, "fsdp", z_shift(1))
    from_above = lax.ppermute(weight, "fsdp", z_shift(-1))
    own = lax.all_gather(weight, "fsdp", axis=0, axis_index_groups=x_rings)

    parts = delta.reshape(rows, Y, columns // Y).transpose(1, 0, 2)
    parts = lax.all_to_all(parts, "replica", 0, 0, axis_index_groups=y_rings)
    summed = jnp.sum(parts.astype(jnp.float32), axis=0)

    others = jnp.stack([from_below, from_above])
    summed, others = lax.optimization_barrier((summed, others))
    right = lax.ppermute(others, "fsdp", x_shift(1))
    left = lax.ppermute(others, "fsdp", x_shift(-1))

    parts = summed.reshape(rows, 8, columns // 64).transpose(1, 0, 2)
    parts = lax.all_to_all(parts, "replica", 0, 0, axis_index_groups=zc_groups)
    new_params, new_momentum = update(jnp.sum(parts, axis=0), params, momentum)
    merged = new_params.astype(jnp.bfloat16)

    along_y = spread(merged, y_rings)
    along_y, right, left = lax.optimization_barrier((along_y, right, left))
    far_below = lax.ppermute(right[:1], "fsdp", x_shift(1))
    far_above = lax.ppermute(left[1:], "fsdp", x_shift(-1))
    merged_weights = assemble(lax.all_gather(along_y, "replica", axis=0, axis_index_groups=z_lines))

    near = (jnp.arange(X, dtype=jnp.int32) * ZH + z).astype(jnp.int32)
    below, above = (z + 2) % ZH, (z + 1) % ZH
    local_blocks = jnp.stack([x * ZH + below, x * ZH + above]).astype(jnp.int32)
    zeros = jnp.zeros((activation.shape[0], weight.shape[1]), jnp.bfloat16)
    keys = project(
        jnp.concatenate([near, local_blocks]), activation, [own, others], zeros, jnp.float32
    )
    blocks = jnp.stack(
        [(x + step) % X * ZH + side for step in (3, 1) for side in (below, above)]
        + [(x + 2) % X * ZH + side for side in (below, above)]
    )
    keys = project(
        blocks.astype(jnp.int32), activation, [right, left, far_below, far_above], keys, jnp.bfloat16
    )
    return new_params, new_momentum, merged_weights, keys[None]


def solution(mesh):
    return jax.shard_map(
        local,
        mesh=mesh,
        in_specs=(
            P("replica", "fsdp", None),
            P("replica", "fsdp", None),
            P("replica", "fsdp", None),
            P("fsdp", "replica"),
            P("fsdp", "replica"),
        ),
        out_specs=(
            P("fsdp", "replica"),
            P("fsdp", "replica"),
            P("fsdp", None),
            P("replica", "fsdp", None),
        ),
        check_vma=False,
    )
```

time: 508 us -> 157 us (0.31)
  waiting for transfers between devices: 387 us -> 46.5 us
  blocking collectives: 81.5 us -> 14.2 us
  starting transfers between devices: 0.08 us -> 63.9 us
  Pallas kernels: 0 us -> 7.37 us
    unnamed x3 -> x1, waiting for transfers between devices: 387 us -> 0.68 us
    all_gather x1, blocking collectives: 81.5 us -> 14.2 us  [local(): lax.all_gather(along_y, 'replica', axis=0, axis_index_groups=z_lines)]
    ppermute x0 -> x7, waiting for transfers between devices: none -> 42.5 us  [the longest x1 22.9 us: local(): from_above = lax.ppermute(weight, 'fsdp', z_shift(-1))]
    ppermute x0 -> x7, starting transfers between devices: none -> 35.7 us  [the longest x1 10.6 us: local(): from_below = lax.ppermute(weight, 'fsdp', z_shift(1))]
    all_to_all x0 -> x3, starting transfers between devices: none -> 28.2 us  [the longest x1 14 us: local(): parts = lax.all_to_all(parts, 'replica', 0, 0, axis_index_groups=zc_groups)]
    unnamed x9 -> x11, local copies, waits for them, and re-layouts: 11.8 us -> 2.87 us
    pallas_call x0 -> x3, Pallas kernels: none -> 7.37 us  [the longest x2 5.25 us: project(): pl.pallas_call(matmul_kernel, grid_spec=pltpu.PrefetchScalarGridSpec(num_...]
  transfers between devices with their start and end apart: 2 -> 11, of which waited for: 1 -> 8; matrix products, arithmetic and copies ran while one was open for 1% -> 4% of each run, Pallas kernels for 0% -> 3%
where the time goes in v1:
time: 157 us
  starting transfers between devices  63.9 us (41%)
  waiting for transfers between devices  46.5 us (30%)
  between operations  14.3 us (9%)
  blocking collectives  14.2 us (9%)
  local copies, waits for them, and re-layouts  9.37 us (6%)
  Pallas kernels  7.37 us (5%)
    ppermute x1, waiting for transfers between devices, local(): from_above = lax.ppermute(weight, 'fsdp', z_shift(-1))  22.9 us
    all_gather x1, blocking collectives, local(): lax.all_gather(along_y, 'replica', axis=0, axis_index_groups=z_lines)  14.2 us
    all_to_all x1, starting transfers between devices, local(): parts = lax.all_to_all(parts, 'replica', 0, 0, axis_index_groups=zc_groups)  14 us
    ppermute x1, starting transfers between devices, local(): from_below = lax.ppermute(weight, 'fsdp', z_shift(1))  10.6 us
    all_to_all x1, starting transfers between devices, local(): parts = lax.all_to_all(parts, 'replica', 0, 0, axis_index_groups=y_rings)  7.65 us
    ppermute x1, waiting for transfers between devices, local(): from_below = lax.ppermute(weight, 'fsdp', z_shift(1))  7.01 us
    all_to_all x1, starting transfers between devices, spread(): return lax.all_to_all(copies, 'replica', 0, 0, axis_index_groups=groups)  6.63 us
    ppermute x1, starting transfers between devices, assemble(): other = lax.ppermute(own, 'replica', cores)  6.38 us
  transfers between devices with their start and end apart: 11, of which 8 were waited for; matrix products, arithmetic and copies ran while one was open for 4% of the time, Pallas kernels for 3%

profile of v1, /device:TPU:1, one launch (start us, length us, event | category | flops | bytes accessed | tf_op | source)
XLA Modules:
  0.0 156.6 jit_solution(11703431098202262322)
XLA Ops:
  7.2 1.4 copy.11
  8.6 0.0 copy-start.2
  8.6 1.2 copy.9
  9.8 7.7 %all-to-all-start = ((bf16[8,16,3584]{2,1,0:T(8,128)(2,1)}), bf16[8,16,3584]{2,1,0:T(8,128)(2,1)S(1)}, u32[]{:S(2)}, u32[]{:S(2)}) async-start(bf16[8,16,3584]{2,1,0:T(8,128)(2,1)} %copy.9), calls=%async_computation | async-start | bytes 1835008 | tf_op jit(solution)/shard_map/all_to_all | solution.py:121
  17.5 0.0 all-gather.3.cloned.1.call-start
  17.5 0.7 all-gather.3.cloned.1.call-update
  18.2 0.0 copy-done.2
  18.2 10.6 %collective-permute-start = (bf16[384,512]{1,0:T(8,128)(2,1)S(1)}, bf16[384,512]{1,0:T(8,128)(2,1)S(1)}, u32[]{:S(2)}, u32[]{:S(2)}) collective-permute-start(bf16[384,512]{1,0:T(8,128)(2,1)S(1)} %bitcast.26), channel_id=1, source_target_pairs={{0,1},{1,2},{2,0},{3,4},{4,5},{5,3},{6,7},{7,8},{8,6},{9,10},{10,1... | collective-permute-start | bytes 1179656 | tf_op jit(solution)/shard_map/ppermute | solution.py:116
  28.9 5.6 %collective-permute-start.1 = (bf16[384,512]{1,0:T(8,128)(2,1)S(1)}, bf16[384,512]{1,0:T(8,128)(2,1)S(1)}, u32[]{:S(2)}, u32[]{:S(2)}) collective-permute-start(bf16[384,512]{1,0:T(8,128)(2,1)S(1)} %bitcast.27), channel_id=1, source_target_pairs={{0,2},{1,0},{2,1},{3,5},{4,3},{5,4},{6,8},{7,6},{8,7},{9,11},{10,9... | collective-permute-start | bytes 1179656 | tf_op jit(solution)/shard_map/ppermute | solution.py:117
  34.4 7.0 %collective-permute-done = bf16[384,512]{1,0:T(8,128)(2,1)S(1)} collective-permute-done((bf16[384,512]{1,0:T(8,128)(2,1)S(1)}, bf16[384,512]{1,0:T(8,128)(2,1)S(1)}, u32[]{:S(2)}, u32[]{:S(2)}) %collective-permute-start) | collective-permute-done | bytes 393248 | tf_op jit(solution)/shard_map/ppermute | solution.py:116
  41.4 22.9 %collective-permute-done.1 = bf16[384,512]{1,0:T(8,128)(2,1)S(1)} collective-permute-done((bf16[384,512]{1,0:T(8,128)(2,1)S(1)}, bf16[384,512]{1,0:T(8,128)(2,1)S(1)}, u32[]{:S(2)}, u32[]{:S(2)}) %collective-permute-start.1) | collective-permute-done | bytes 393248 | tf_op jit(solution)/shard_map/ppermute | solution.py:117
  64.3 0.1 pad_maximum_fusion.refs_1_
  64.4 0.0 copy-start.3
  64.4 0.0 copy-start.4
  64.4 0.0 all-to-all-done
  64.5 0.1 convert_reduce_fusion
  64.6 0.1 reshape.11
  64.7 0.9 copy.10
  65.6 14.0 %all-to-all-start.1 = ((f32[8,16,448]{2,1,0:T(8,128)}), f32[8,16,448]{2,1,0:T(8,128)S(1)}, u32[]{:S(2)}, u32[]{:S(2)}) async-start(f32[8,16,448]{2,1,0:T(8,128)} %copy.10), calls=%async_computation.1 | async-start | bytes 524288 | tf_op jit(solution)/shard_map/all_to_all | solution.py:130
  79.5 0.0 copy-start
  79.5 3.2 %collective-permute-start.2 = (bf16[2,384,512]{2,1,0:T(8,128)(2,1)S(1)}, bf16[2,384,512]{2,1,0:T(8,128)(2,1)}, u32[]{:S(2)}, u32[]{:S(2)}) collective-permute-start(bf16[2,384,512]{2,1,0:T(8,128)(2,1)S(1)} %pad_maximum_fusion.refs_1_), channel_id=1, source_target_pairs={{0,3},{1,4},{2,5},{3,6},{4,7},{5,8},{6,9},{7,10},{8,11},{9,0},{10,... | collective-permute-start | bytes 2359304 | tf_op jit(solution)/shard_map/ppermute | solution.py:126
  82.8 3.4 %collective-permute-start.3 = (bf16[2,384,512]{2,1,0:T(8,128)(2,1)S(1)}, bf16[2,384,512]{2,1,0:T(8,128)(2,1)}, u32[]{:S(2)}, u32[]{:S(2)}) collective-permute-start(bf16[2,384,512]{2,1,0:T(8,128)(2,1)S(1)} %pad_maximum_fusion.refs_1_), channel_id=1, source_target_pairs={{0,9},{1,10},{2,11},{3,0},{4,1},{5,2},{6,3},{7,4},{8,5},{9,6},{10,... | collective-permute-start | bytes 2359304 | tf_op jit(solution)/shard_map/ppermute | solution.py:127
  86.2 2.5 %all-to-all-done.1 = f32[8,16,448]{2,1,0:T(8,128)S(1)} async-done(((f32[8,16,448]{2,1,0:T(8,128)}), f32[8,16,448]{2,1,0:T(8,128)S(1)}, u32[]{:S(2)}, u32[]{:S(2)}) %all-to-all-start.1) | async-done | bytes 229408 | tf_op jit(solution)/shard_map/all_to_all | solution.py:130
  88.7 0.0 copy-done.3
  88.7 0.0 copy-done.4
  88.7 0.6 fusion
  89.3 0.7 broadcast_in_dim.13
  90.0 6.6 %all-to-all-start.2 = ((bf16[8,16,448]{2,1,0:T(8,128)(2,1)}), bf16[8,16,448]{2,1,0:T(8,128)(2,1)S(1)}, u32[]{:S(2)}, u32[]{:S(2)}) async-start(bf16[8,16,448]{2,1,0:T(8,128)(2,1)} %broadcast_in_dim.13), calls=%async_computation.2 | async-start | bytes 262144 | tf_op jit(solution)/shard_map/all_to_all | solution.py:33
  96.6 5.4 %collective-permute-done.2.refs_0_ = bf16[2,384,512]{2,1,0:T(8,128)(2,1)} collective-permute-done((bf16[2,384,512]{2,1,0:T(8,128)(2,1)S(1)}, bf16[2,384,512]{2,1,0:T(8,128)(2,1)}, u32[]{:S(2)}, u32[]{:S(2)}) %collective-permute-start.2) | collective-permute-done | bytes 786464 | tf_op jit(solution)/shard_map/ppermute | solution.py:126
  102.0 1.6 %collective-permute-done.3.refs_1_ = bf16[2,384,512]{2,1,0:T(8,128)(2,1)} collective-permute-done((bf16[2,384,512]{2,1,0:T(8,128)(2,1)S(1)}, bf16[2,384,512]{2,1,0:T(8,128)(2,1)}, u32[]{:S(2)}, u32[]{:S(2)}) %collective-permute-start.3) | collective-permute-done | bytes 786464 | tf_op jit(solution)/shard_map/ppermute | solution.py:127
  103.6 0.8 all-to-all-done.2
  104.4 14.2 %all-gather = bf16[32,16,448]{2,1,0:T(8,128)(2,1)} all-gather(bf16[8,16,448]{2,1,0:T(8,128)(2,1)S(1)} %all-to-all-done.2), channel_id=2, replica_groups={{0,24,48,72},{12,36,60,84},{96,120,144,168},{108,132,156,180},{192,216,..., dimensions={0}, use_global_device_ids=true | all-gather | bytes 573440 | tf_op jit(solution)/shard_map/all_gather | solution.py:138
  118.6 6.4 %collective-permute-start.4 = (bf16[4,8,16,448]{3,2,1,0:T(8,128)(2,1)}, bf16[4,8,16,448]{3,2,1,0:T(8,128)(2,1)}, u32[]{:S(2)}, u32[]{:S(2)}) collective-permute-start(bf16[4,8,16,448]{3,2,1,0:T(8,128)(2,1)} %bitcast.6.own_ref), channel_id=1, source_target_pairs={{0,12},{12,0},{24,36},{36,24},{48,60},{60,48},{72,84},{84,72},{96,... | collective-permute-start | bytes 1376264 | tf_op jit(solution)/shard_map/ppermute | solution.py:97
  125.0 1.8 %slice.6 = bf16[1,384,512]{2,1,0:T(8,128)(2,1)} slice(bf16[2,384,512]{2,1,0:T(8,128)(2,1)} %collective-permute-done.2.refs_0_), slice={[0:1], [0:384], [0:512]} | slice | bytes 786432 | tf_op jit(solution)/shard_map/slice | solution.py:136
  126.7 3.0 %collective-permute-start.5 = (bf16[1,384,512]{2,1,0:T(8,128)(2,1)}, bf16[1,384,512]{2,1,0:T(8,128)(2,1)S(1)}, u32[]{:S(2)}, u32[]{:S(2)}) collective-permute-start(bf16[1,384,512]{2,1,0:T(8,128)(2,1)} %slice.6), channel_id=1, source_target_pairs={{0,3},{1,4},{2,5},{3,6},{4,7},{5,8},{6,9},{7,10},{8,11},{9,0},{10,... | collective-permute-start | bytes 1179656 | tf_op jit(solution)/shard_map/ppermute | solution.py:136
  129.8 1.8 %slice.7 = bf16[1,384,512]{2,1,0:T(8,128)(2,1)} slice(bf16[2,384,512]{2,1,0:T(8,128)(2,1)} %collective-permute-done.3.refs_1_), slice={[1:2], [0:384], [0:512]} | slice | bytes 786432 | tf_op jit(solution)/shard_map/slice | solution.py:137
  131.6 3.4 %collective-permute-start.6 = (bf16[1,384,512]{2,1,0:T(8,128)(2,1)}, bf16[1,384,512]{2,1,0:T(8,128)(2,1)}, u32[]{:S(2)}, u32[]{:S(2)}) collective-permute-start(bf16[1,384,512]{2,1,0:T(8,128)(2,1)} %slice.7), channel_id=1, source_target_pairs={{0,9},{1,10},{2,11},{3,0},{4,1},{5,2},{6,3},{7,4},{8,5},{9,6},{10,... | collective-permute-start | bytes 1179656 | tf_op jit(solution)/shard_map/ppermute | solution.py:137
  135.2 0.1 stack.45.block_ref
  135.2 0.1 pad_add_fusion.block_ref
  135.4 0.0 copy-done
  135.4 0.0 copy-start.1
  135.4 1.4 copy-done.1
  136.8 1.8 %shard_map.85.start_ref = f32[224,512]{1,0:T(8,128)S(1)} custom-call(s32[6]{0:T(128)S(1)} %pad_add_fusion.block_ref, bf16[224,4608]{1,0:T(8,128)(2,1)S(1)} %bitcast.21, bf16[224,512]{1,0:T(8,128)(2,1)S(1)} %broadcast_in_dim.14.start_ref, bf16[4,384,512]{2,1,0:T(8,128)(2,1)S(1)} %copy-done.1, bf16[2,384,512]{2,1,0:T(8,128)(2,1)S(1)} %pad_maximum_fusion.refs_1_), custom_call_target="tpu_custom_call" | custom-call | flops 528482304 | bytes 5111808 | tf_op jit(solution)/shard_map/pallas_call | solution.py:57
  138.6 2.2 %collective-permute-done.5.refs_2_ = bf16[1,384,512]{2,1,0:T(8,128)(2,1)S(1)} collective-permute-done((bf16[1,384,512]{2,1,0:T(8,128)(2,1)}, bf16[1,384,512]{2,1,0:T(8,128)(2,1)S(1)}, u32[]{:S(2)}, u32[]{:S(2)}) %collective-permute-start.5) | collective-permute-done | bytes 393248 | tf_op jit(solution)/shard_map/ppermute | solution.py:136
  140.8 3.4 %collective-permute-done.6.refs_3_ = bf16[1,384,512]{2,1,0:T(8,128)(2,1)} collective-permute-done((bf16[1,384,512]{2,1,0:T(8,128)(2,1)}, bf16[1,384,512]{2,1,0:T(8,128)(2,1)}, u32[]{:S(2)}, u32[]{:S(2)}) %collective-permute-start.6) | collective-permute-done | bytes 393248 | tf_op jit(solution)/shard_map/ppermute | solution.py:137
  144.2 3.4 %shard_map.86 = bf16[224,512]{1,0:T(8,128)(2,1)} custom-call(s32[6]{0:T(128)S(1)} %stack.45.block_ref, bf16[224,4608]{1,0:T(8,128)(2,1)S(1)} %bitcast.22, f32[224,512]{1,0:T(8,128)S(1)} %shard_map.85.start_ref, bf16[2,384,512]{2,1,0:T(8,128)(2,1)} %collective-permute-done.2.refs_0_, bf16[2,384,512]{2,1,0:T(8,128)(2,1)} %collective-permute-done.3.refs_1_, ...), custom_call_target="tpu_custom_call" | custom-call | flops 528482304 | bytes 5111808 | tf_op jit(solution)/shard_map/pallas_call | solution.py:57
  147.6 0.0 collective-permute-done.4.other_ref
  147.6 2.1 %shard_map.84 = bf16[16,28672]{1,0:T(8,128)(2,1)} custom-call(s32[1]{0:T(128)} %bitcast.5.core_ref, bf16[4,8,16,448]{3,2,1,0:T(8,128)(2,1)} %bitcast.6.own_ref, bf16[4,8,16,448]{3,2,1,0:T(8,128)(2,1)} %collective-permute-done.4.other_ref), custom_call_target="tpu_custom_call" | custom-call | tf_op jit(solution)/shard_map/pallas_call | solution.py:100
  (4 shorter events, 0.0 us)
Async XLA Ops:
  8.6 9.6 %copy-start.2 = (bf16[1,384,512]{2,1,0:T(8,128)(2,1)S(1)}, bf16[1,384,512]{2,1,0:T(8,128)(2,1)}, u32[]{:S(2)}) copy-start(bf16[1,384,512]{2,1,0:T(8,128)(2,1)} %param.6) | copy-start | bytes 1179652
  9.8 54.6 %all-to-all-start = ((bf16[8,16,3584]{2,1,0:T(8,128)(2,1)}), bf16[8,16,3584]{2,1,0:T(8,128)(2,1)S(1)}, u32[]{:S(2)}, u32[]{:S(2)}) async-start(bf16[8,16,3584]{2,1,0:T(8,128)(2,1)} %copy.9), calls=%async_computation | async-start | bytes 1835008 | tf_op jit(solution)/shard_map/all_to_all | solution.py:121
  17.5 117.9 %all-gather.3.cloned.1.call-start = ((), (), s32[]{:S(2)}) async-start(), calls=%async_computation.3 | async-start | bytes 1966080 | tf_op jit(solution)/shard_map/all_gather | solution.py:118
  18.2 23.2 %collective-permute-start = (bf16[384,512]{1,0:T(8,128)(2,1)S(1)}, bf16[384,512]{1,0:T(8,128)(2,1)S(1)}, u32[]{:S(2)}, u32[]{:S(2)}) collective-permute-start(bf16[384,512]{1,0:T(8,128)(2,1)S(1)} %bitcast.26), channel_id=1, source_target_pairs={{0,1},{1,2},{2,0},{3,4},{4,5},{5,3},{6,7},{7,8},{8,6},{9,10},{10,1... | collective-permute-start | bytes 1179656 | tf_op jit(solution)/shard_map/ppermute | solution.py:116
  28.9 35.5 %collective-permute-start.1 = (bf16[384,512]{1,0:T(8,128)(2,1)S(1)}, bf16[384,512]{1,0:T(8,128)(2,1)S(1)}, u32[]{:S(2)}, u32[]{:S(2)}) collective-permute-start(bf16[384,512]{1,0:T(8,128)(2,1)S(1)} %bitcast.27), channel_id=1, source_target_pairs={{0,2},{1,0},{2,1},{3,5},{4,3},{5,4},{6,8},{7,6},{8,7},{9,11},{10,9... | collective-permute-start | bytes 1179656 | tf_op jit(solution)/shard_map/ppermute | solution.py:117
  64.4 24.3 %copy-start.3 = (f32[16,448]{1,0:T(8,128)S(1)}, f32[16,448]{1,0:T(8,128)}, u32[]{:S(2)}) copy-start(f32[16,448]{1,0:T(8,128)} %param.8) | copy-start | bytes 86020
  64.4 24.3 %copy-start.4 = (f32[16,448]{1,0:T(8,128)S(1)}, f32[16,448]{1,0:T(8,128)}, u32[]{:S(2)}) copy-start(f32[16,448]{1,0:T(8,128)} %param.9) | copy-start | bytes 86020
  65.6 23.1 %all-to-all-start.1 = ((f32[8,16,448]{2,1,0:T(8,128)}), f32[8,16,448]{2,1,0:T(8,128)S(1)}, u32[]{:S(2)}, u32[]{:S(2)}) async-start(f32[8,16,448]{2,1,0:T(8,128)} %copy.10), calls=%async_computation.1 | async-start | bytes 524288 | tf_op jit(solution)/shard_map/all_to_all | solution.py:130
  79.5 55.8 %copy-start = (bf16[1,224,4608]{2,1,0:T(8,128)(2,1)S(1)}, bf16[1,224,4608]{2,1,0:T(8,128)(2,1)}, u32[]{:S(2)}) copy-start(bf16[1,224,4608]{2,1,0:T(8,128)(2,1)} %param.5) | copy-start | bytes 6193156
  79.5 22.5 %collective-permute-start.2 = (bf16[2,384,512]{2,1,0:T(8,128)(2,1)S(1)}, bf16[2,384,512]{2,1,0:T(8,128)(2,1)}, u32[]{:S(2)}, u32[]{:S(2)}) collective-permute-start(bf16[2,384,512]{2,1,0:T(8,128)(2,1)S(1)} %pad_maximum_fusion.refs_1_), channel_id=1, source_target_pairs={{0,3},{1,4},{2,5},{3,6},{4,7},{5,8},{6,9},{7,10},{8,11},{9,0},{10,... | collective-permute-start | bytes 2359304 | tf_op jit(solution)/shard_map/ppermute | solution.py:126
  82.8 20.8 %collective-permute-start.3 = (bf16[2,384,512]{2,1,0:T(8,128)(2,1)S(1)}, bf16[2,384,512]{2,1,0:T(8,128)(2,1)}, u32[]{:S(2)}, u32[]{:S(2)}) collective-permute-start(bf16[2,384,512]{2,1,0:T(8,128)(2,1)S(1)} %pad_maximum_fusion.refs_1_), channel_id=1, source_target_pairs={{0,9},{1,10},{2,11},{3,0},{4,1},{5,2},{6,3},{7,4},{8,5},{9,6},{10,... | collective-permute-start | bytes 2359304 | tf_op jit(solution)/shard_map/ppermute | solution.py:127
  90.0 14.4 %all-to-all-start.2 = ((bf16[8,16,448]{2,1,0:T(8,128)(2,1)}), bf16[8,16,448]{2,1,0:T(8,128)(2,1)S(1)}, u32[]{:S(2)}, u32[]{:S(2)}) async-start(bf16[8,16,448]{2,1,0:T(8,128)(2,1)} %broadcast_in_dim.13), calls=%async_computation.2 | async-start | bytes 262144 | tf_op jit(solution)/shard_map/all_to_all | solution.py:33
  118.6 29.1 %collective-permute-start.4 = (bf16[4,8,16,448]{3,2,1,0:T(8,128)(2,1)}, bf16[4,8,16,448]{3,2,1,0:T(8,128)(2,1)}, u32[]{:S(2)}, u32[]{:S(2)}) collective-permute-start(bf16[4,8,16,448]{3,2,1,0:T(8,128)(2,1)} %bitcast.6.own_ref), channel_id=1, source_target_pairs={{0,12},{12,0},{24,36},{36,24},{48,60},{60,48},{72,84},{84,72},{96,... | collective-permute-start | bytes 1376264 | tf_op jit(solution)/shard_map/ppermute | solution.py:97
  126.7 14.0 %collective-permute-start.5 = (bf16[1,384,512]{2,1,0:T(8,128)(2,1)}, bf16[1,384,512]{2,1,0:T(8,128)(2,1)S(1)}, u32[]{:S(2)}, u32[]{:S(2)}) collective-permute-start(bf16[1,384,512]{2,1,0:T(8,128)(2,1)} %slice.6), channel_id=1, source_target_pairs={{0,3},{1,4},{2,5},{3,6},{4,7},{5,8},{6,9},{7,10},{8,11},{9,0},{10,... | collective-permute-start | bytes 1179656 | tf_op jit(solution)/shard_map/ppermute | solution.py:136
  131.6 12.6 %collective-permute-start.6 = (bf16[1,384,512]{2,1,0:T(8,128)(2,1)}, bf16[1,384,512]{2,1,0:T(8,128)(2,1)}, u32[]{:S(2)}, u32[]{:S(2)}) collective-permute-start(bf16[1,384,512]{2,1,0:T(8,128)(2,1)} %slice.7), channel_id=1, source_target_pairs={{0,9},{1,10},{2,11},{3,0},{4,1},{5,2},{6,3},{7,4},{8,5},{9,6},{10,... | collective-permute-start | bytes 1179656 | tf_op jit(solution)/shard_map/ppermute | solution.py:137
  135.4 1.4 copy-start.1
Sparse Core Ops, SparseCore 0:
  20.7 41.6 all-gather.2

commit v2 on v1

--- a/solution.py
+++ b/solution.py
@@ -40,7 +40,7 @@
     for weight_ref in weight_refs:
         count, depth, _ = weight_ref.shape
         for part in range(count):
-            columns = pl.ds(pl.multiple_of(block_ref[index] * depth, 128), depth)
+            columns = pl.ds(pl.multiple_of(block_ref[index] * 128, 128), depth)
             total += jnp.dot(
                 token_ref[:, columns], weight_ref[part], preferred_element_type=jnp.float32
             )
@@ -48,7 +48,7 @@
     out_ref[...] = total.astype(out_ref.dtype)
 
 
-def project(blocks, activation, weights, start, dtype):
+def project(blocks, activation, weights, start, dtype, weigh=1):
     tokens, features = activation.shape
     width = weights[0].shape[-1]
     tile = width // 2
@@ -65,11 +65,10 @@
         ),
         out_shape=jax.ShapeDtypeStruct((tokens, width), dtype),
         cost_estimate=pl.CostEstimate(
-            flops=2 * depth * tokens * width,
+            flops=2 * depth * tokens * width * weigh,
             bytes_accessed=2 * depth * width + 2 * tokens * features + 6 * tokens * width,
             transcendentals=0,
         ),
-        compiler_params=pltpu.CompilerParams(vmem_limit_bytes=32 * 2**20),
     )(blocks, activation, start, *weights)
 
 
@@ -80,32 +79,50 @@
     return new_params, new_momentum
 
 
+def pair_kernel(first_ref, second_ref, out_ref):
+    out_ref[0] = first_ref[...]
+    out_ref[1] = second_ref[...]
+
+
+def pair(first, second):
+    rows, width = first.shape
+    part = pl.BlockSpec((rows // 2, width), lambda i: (i, 0))
+    return pl.pallas_call(
+        pair_kernel,
+        grid=(2,),
+        in_specs=[part, part],
+        out_specs=pl.BlockSpec((2, rows // 2, width), lambda i: (0, i, 0)),
+        out_shape=jax.ShapeDtypeStruct((2, rows, width), first.dtype),
+        cost_estimate=pl.CostEstimate(
+            flops=4 * 10**10, bytes_accessed=8 * rows * width, transcendentals=0
+        ),
+    )(first, second)
+
+
 def assemble_kernel(core_ref, own_ref, other_ref, out_ref):
-    zs, ys, _, width = own_ref.shape
+    chips, _, width = own_ref.shape
     even = core_ref[0] == 0
-    for y in range(ys):
-        for z in range(zs):
-            own, other = own_ref[z, y], other_ref[z, y]
-            at = (y * zs + z) * 2 * width
-            out_ref[:, at : at + 2 * width] = jnp.concatenate(
-                [jnp.where(even, own, other), jnp.where(even, other, own)], axis=1
-            )
+    for chip in range(chips):
+        own, other = own_ref[chip], other_ref[chip]
+        out_ref[:, 2 * chip * width : 2 * (chip + 1) * width] = jnp.concatenate(
+            [jnp.where(even, own, other), jnp.where(even, other, own)], axis=1
+        )
 
 
 def assemble(own):
-    zs, ys, rows, width = own.shape
+    chips, rows, width = own.shape
     other = lax.ppermute(own, "replica", cores)
     core = (lax.axis_index("replica") % 2).astype(jnp.int32)[None]
-    part = pl.BlockSpec((zs, ys // 2, rows, width), lambda y, c: (0, y, 0, 0))
+    part = pl.BlockSpec((chips // 2, rows, width), lambda i, c: (i, 0, 0))
     return pl.pallas_call(
         assemble_kernel,
         grid_spec=pltpu.PrefetchScalarGridSpec(
             num_scalar_prefetch=1,
             grid=(2,),
             in_specs=[part, part],
-            out_specs=pl.BlockSpec((rows, zs * ys * width), lambda y, c: (0, y)),
+            out_specs=pl.BlockSpec((rows, chips * width), lambda i, c: (0, i)),
         ),
-        out_shape=jax.ShapeDtypeStruct((rows, zs * ys * 2 * width), own.dtype),
+        out_shape=jax.ShapeDtypeStruct((rows, chips * 2 * width), own.dtype),
     )(core, own, other)
 
 def local(tokens, key_weight, deltas, params, momentum):
@@ -113,44 +130,33 @@
     x, z = lax.axis_index("fsdp") // ZH, lax.axis_index("fsdp") % ZH
     rows, columns = delta.shape
 
+    own = lax.all_gather(weight, "fsdp", axis=0, axis_index_groups=x_rings)
     from_below = lax.ppermute(weight, "fsdp", z_shift(1))
     from_above = lax.ppermute(weight, "fsdp", z_shift(-1))
-    own = lax.all_gather(weight, "fsdp", axis=0, axis_index_groups=x_rings)
+    starts = jnp.arange(X, dtype=jnp.int32)[:, None] * ZH
+    zeros = jnp.zeros((activation.shape[0], weight.shape[1]), jnp.bfloat16)
+    near = (starts + z).astype(jnp.int32)
+    keys = project(near.ravel() * 3, activation, [own], zeros, jnp.float32)
 
     parts = delta.reshape(rows, Y, columns // Y).transpose(1, 0, 2)
     parts = lax.all_to_all(parts, "replica", 0, 0, axis_index_groups=y_rings)
+
+    from_below, from_above, keys = lax.optimization_barrier((from_below, from_above, keys))
+    others = pair(from_below, from_above)
+    parts, others = lax.optimization_barrier((parts, others))
     summed = jnp.sum(parts.astype(jnp.float32), axis=0)
-
-    others = jnp.stack([from_below, from_above])
-    summed, others = lax.optimization_barrier((summed, others))
-    right = lax.ppermute(others, "fsdp", x_shift(1))
-    left = lax.ppermute(others, "fsdp", x_shift(-1))
+    rest = lax.all_gather(others, "fsdp", axis=0, axis_index_groups=x_rings)
 
     parts = summed.reshape(rows, 8, columns // 64).transpose(1, 0, 2)
     parts = lax.all_to_all(parts, "replica", 0, 0, axis_index_groups=zc_groups)
     new_params, new_momentum = update(jnp.sum(parts, axis=0), params, momentum)
     merged = new_params.astype(jnp.bfloat16)
 
-    along_y = spread(merged, y_rings)
-    along_y, right, left = lax.optimization_barrier((along_y, right, left))
-    far_below = lax.ppermute(right[:1], "fsdp", x_shift(1))
-    far_above = lax.ppermute(left[1:], "fsdp", x_shift(-1))
-    merged_weights = assemble(lax.all_gather(along_y, "replica", axis=0, axis_index_groups=z_lines))
+    merged_weights = assemble(spread(merged, same_core))
 
-    near = (jnp.arange(X, dtype=jnp.int32) * ZH + z).astype(jnp.int32)
-    below, above = (z + 2) % ZH, (z + 1) % ZH
-    local_blocks = jnp.stack([x * ZH + below, x * ZH + above]).astype(jnp.int32)
-    zeros = jnp.zeros((activation.shape[0], weight.shape[1]), jnp.bfloat16)
-    keys = project(
-        jnp.concatenate([near, local_blocks]), activation, [own, others], zeros, jnp.float32
-    )
-    blocks = jnp.stack(
-        [(x + step) % X * ZH + side for step in (3, 1) for side in (below, above)]
-        + [(x + 2) % X * ZH + side for side in (below, above)]
-    )
-    keys = project(
-        blocks.astype(jnp.int32), activation, [right, left, far_below, far_above], keys, jnp.bfloat16
-    )
+    far = (starts + jnp.stack([(z + 2) % ZH, (z + 1) % ZH])).astype(jnp.int32)
+    rest = rest.reshape((-1,) + weight.shape)
+    keys = project(far.ravel() * 3, activation, [rest], keys, jnp.bfloat16)
     return new_params, new_momentum, merged_weights, keys[None]
 
 

time: 157 us -> 128 us (0.82)
  starting transfers between devices: 63.9 us -> 28.6 us
  blocking collectives: 14.2 us -> 44.2 us
  waiting for transfers between devices: 46.5 us -> 19 us
  Pallas kernels: 7.37 us -> 13 us
  local copies, waits for them, and re-layouts: 9.37 us -> 6.56 us
    all_to_all x0 -> x2, blocking collectives: none -> 44.2 us  [the longest x1 23.6 us: spread(): return lax.all_to_all(copies, 'replica', 0, 0, axis_index_groups=groups)]
    ppermute x1, waiting for transfers between devices: 22.9 us -> 0.01 us  [local(): from_above = lax.ppermute(weight, 'fsdp', z_shift(-1))]
    all_to_all x2 -> x0, starting transfers between devices: 20.6 us -> none  [the longest x1 14 us: local(): parts = lax.all_to_all(parts, 'replica', 0, 0, axis_index_groups=zc_groups)]
    all_gather x1, waiting for transfers between devices: 0.01 us -> 17.6 us  [local(): own = lax.all_gather(weight, 'fsdp', axis=0, axis_index_groups=x_rings)]
    all_gather x1 -> x0, blocking collectives: 14.2 us -> none  [local(): lax.all_gather(along_y, 'replica', axis=0, axis_index_groups=z_lines)]
    ppermute x4 -> x0, starting transfers between devices: 13.1 us -> none  [the longest x1 3.43 us: local(): far_above = lax.ppermute(left[1:], 'fsdp', x_shift(-1))]
    ppermute x4 -> x0, waiting for transfers between devices: 12.6 us -> none  [the longest x1 5.4 us: local(): right = lax.ppermute(others, 'fsdp', x_shift(1))]
    ppermute x1, starting transfers between devices: 5.56 us -> 15.1 us  [local(): from_above = lax.ppermute(weight, 'fsdp', z_shift(-1))]
  transfers between devices with their start and end apart: 11 -> 6, of which waited for: 8 -> 2; matrix products, arithmetic and copies ran while one was open for 4% -> 5% of each run, Pallas kernels for 3% -> 6%
where the time goes in v2:
time: 128 us; the launch traced here: 127 us
  blocking collectives  44.2 us (35%)
  starting transfers between devices  28.6 us (22%)
  waiting for transfers between devices  19 us (15%)
  between operations  14.2 us (11%)
  Pallas kernels  13 us (10%)
  local copies, waits for them, and re-layouts  6.56 us (5%)
  other arithmetic  1.47 us (1%)
    all_to_all x1, blocking collectives, spread(): return lax.all_to_all(copies, 'replica', 0, 0, axis_index_groups=groups)  23.6 us
    all_to_all x1, blocking collectives, local(): parts = lax.all_to_all(parts, 'replica', 0, 0, axis_index_groups=zc_groups)  20.5 us
    all_gather x1, waiting for transfers between devices, local(): own = lax.all_gather(weight, 'fsdp', axis=0, axis_index_groups=x_rings)  17.6 us
    ppermute x1, starting transfers between devices, local(): from_above = lax.ppermute(weight, 'fsdp', z_shift(-1))  15.1 us
    pallas_call x2, Pallas kernels, project(): pl.pallas_call(matmul_kernel, grid_spec=pltpu.PrefetchScalarGridSpec(num_...  8.89 us
    all_to_all x1, starting transfers between devices, local(): parts = lax.all_to_all(parts, 'replica', 0, 0, axis_index_groups=y_rings)  6.82 us
    ppermute x1, starting transfers between devices, assemble(): other = lax.ppermute(own, 'replica', cores)  4.72 us
    unnamed x13, local copies, waits for them, and re-layouts  3.76 us
  transfers between devices with their start and end apart: 6, of which 2 were waited for; matrix products, arithmetic and copies ran while one was open for 5% of the time, Pallas kernels for 6%

profile of v2, /device:TPU:1, one launch (start us, length us, event | category | flops | bytes accessed | tf_op | source)
XLA Modules:
  0.0 127.0 jit_solution(8241640092585038916)
XLA Ops:
  7.2 0.0 all-gather.4.cloned.1.call-start
  7.2 0.7 all-gather.4.cloned.1.call-update
  7.9 15.1 %collective-permute-start.1 = (bf16[384,512]{1,0:T(8,128)(2,1)}, bf16[384,512]{1,0:T(8,128)(2,1)S(1)}, u32[]{:S(2)}, u32[]{:S(2)}) collective-permute-start(bf16[384,512]{1,0:T(8,128)(2,1)} %bitcast.17), channel_id=1, source_target_pairs={{0,2},{1,0},{2,1},{3,5},{4,3},{5,4},{6,8},{7,6},{8,7},{9,11},{10,9... | collective-permute-start | bytes 1179656 | tf_op jit(solution)/shard_map/ppermute | solution.py:135
  23.0 1.9 %collective-permute-start = (bf16[384,512]{1,0:T(8,128)(2,1)}, bf16[384,512]{1,0:T(8,128)(2,1)S(1)}, u32[]{:S(2)}, u32[]{:S(2)}) collective-permute-start(bf16[384,512]{1,0:T(8,128)(2,1)} %bitcast.18), channel_id=1, source_target_pairs={{0,1},{1,2},{2,0},{3,4},{4,5},{5,3},{6,7},{7,8},{8,6},{9,10},{10,1... | collective-permute-start | bytes 1179656 | tf_op jit(solution)/shard_map/ppermute | solution.py:134
  24.9 1.4 %copy.11 = bf16[2,8,8,3584]{3,2,1,0:T(8,128)(2,1)S(1)} copy(bf16[2,8,8,3584]{3,1,2,0:T(8,128)(2,1)} %bitcast.16) | data formatting | bytes 1835008
  26.4 1.2 copy.9
  27.6 6.8 %all-to-all-start = ((bf16[8,16,3584]{2,1,0:T(8,128)(2,1)}), bf16[8,16,3584]{2,1,0:T(8,128)(2,1)S(1)}, u32[]{:S(2)}, u32[]{:S(2)}) async-start(bf16[8,16,3584]{2,1,0:T(8,128)(2,1)} %copy.9), calls=%async_computation | async-start | bytes 1835008 | tf_op jit(solution)/shard_map/all_to_all | solution.py:142
  34.4 0.0 all-gather.6.cloned.1.call-start
  34.5 0.5 add_multiply_fusion.1.block_ref
  35.0 17.6 %all-gather.4.cloned.1.call-done.refs_0_ = bf16[4,384,512]{2,1,0:T(8,128)(2,1)} async-done(((bf16[1,384,512]{2,1,0:T(8,128)(2,1)}), bf16[4,384,512]{2,1,0:T(8,128)(2,1)}) %all-gather.4.cloned.1.call-update) | async-done | bytes 1572880 | tf_op jit(solution)/shard_map/all_gather | solution.py:133
  52.6 0.7 broadcast_in_dim.14.start_ref
  53.3 4.1 %shard_map.84.start_ref = f32[224,512]{1,0:T(8,128)} custom-call(s32[4]{0:T(128)} %add_multiply_fusion.1.block_ref, bf16[224,4608]{1,0:T(8,128)(2,1)} %bitcast.12, bf16[224,512]{1,0:T(8,128)(2,1)} %broadcast_in_dim.14.start_ref, bf16[4,384,512]{2,1,0:T(8,128)(2,1)} %all-gather.4.cloned.1.call-done.refs_0_), custom_call_target="tpu_custom_call" | custom-call | flops 352321536 | bytes 4325376 | tf_op jit(solution)/shard_map/pallas_call | solution.py:57
  57.3 0.0 collective-permute-done.1.second_ref
  57.4 0.0 copy-start.4
  57.4 0.0 collective-permute-done.first_ref
  57.4 0.7 copy-done.4
  58.1 0.0 copy-start.5
  58.1 0.8 copy-done.5
  58.9 2.0 %shard_map.85 = bf16[2,384,512]{2,1,0:T(8,128)(2,1)} custom-call(bf16[384,512]{1,0:T(8,128)(2,1)} %copy-done.5, bf16[384,512]{1,0:T(8,128)(2,1)} %copy-done.4), custom_call_target="tpu_custom_call" | custom-call | flops 40000000000 | bytes 1572864 | tf_op jit(solution)/shard_map/pallas_call | solution.py:90
  60.9 0.0 copy-start.2
  60.9 0.0 copy-start.3
  60.9 0.0 all-to-all-done
  60.9 0.0 all-gather.6.cloned.1.call-update
  60.9 0.1 convert_reduce_fusion
  61.0 0.1 reshape.29
  61.2 0.2 copy.10
  61.3 20.5 %all_to_all.15 = f32[8,16,448]{2,1,0:T(8,128)S(1)} all-to-all(f32[8,16,448]{2,1,0:T(8,128)S(1)} %copy.10), channel_id=1, replica_groups={{0,12,24,36,48,60,72,84},{96,108,120,132,144,156,168,180},{192,204,216,..., dimensions={0} | all-to-all | bytes 458752 | tf_op jit(solution)/shard_map/all_to_all | solution.py:151
  81.9 0.0 copy-done.2
  81.9 0.0 copy-done.3
  81.9 0.6 fusion
  82.6 23.6 %all_to_all.16.own_ref = bf16[32,16,448]{2,1,0:T(8,128)(2,1)S(1)} all-to-all(bf16[32,16,448]{2,1,0:T(8,128)(2,1)S(1)} %broadcast_in_dim.16), channel_id=1, replica_groups={{0,24,48,72,96,120,144,168,192,216,240,264,288,312,336,360,384,408,432,..., dimensions={0} | all-to-all | bytes 917504 | tf_op jit(solution)/shard_map/all_to_all | solution.py:33
  106.2 0.0 copy-start
  106.2 4.7 %collective-permute-start.2 = (bf16[32,16,448]{2,1,0:T(8,128)(2,1)S(1)}, bf16[32,16,448]{2,1,0:T(8,128)(2,1)S(1)}, u32[]{:S(2)}, u32[]{:S(2)}) collective-permute-start(bf16[32,16,448]{2,1,0:T(8,128)(2,1)S(1)} %all_to_all.16.own_ref), channel_id=1, source_target_pairs={{0,12},{12,0},{24,36},{36,24},{48,60},{60,48},{72,84},{84,72},{96,... | collective-permute-start | bytes 1376264 | tf_op jit(solution)/shard_map/ppermute | solution.py:114
  111.0 0.1 pad_add_fusion
  111.1 0.1 add_multiply_fusion
  111.2 0.6 mul.39.block_ref
  111.7 0.7 collective-permute-done.2.other_ref
  112.5 0.0 copy-start.1
  112.5 0.0 copy-done
  112.5 0.8 copy-done.1
  113.3 2.1 %shard_map.86 = bf16[16,28672]{1,0:T(8,128)(2,1)} custom-call(s32[1]{0:T(128)} %bitcast.4.core_ref, bf16[32,16,448]{2,1,0:T(8,128)(2,1)} %copy-done, bf16[32,16,448]{2,1,0:T(8,128)(2,1)} %copy-done.1), custom_call_target="tpu_custom_call" | custom-call | tf_op jit(solution)/shard_map/pallas_call | solution.py:117
  115.4 0.0 all-gather.6.cloned.1.call-done.refs_0_
  115.4 4.8 %shard_map.87 = bf16[224,512]{1,0:T(8,128)(2,1)} custom-call(s32[8]{0:T(128)} %mul.39.block_ref, bf16[224,4608]{1,0:T(8,128)(2,1)} %bitcast.13, f32[224,512]{1,0:T(8,128)} %shard_map.84.start_ref, bf16[8,384,512]{2,1,0:T(8,128)(2,1)} %all-gather.6.cloned.1.call-done.refs_0_), custom_call_target="tpu_custom_call" | custom-call | flops 704643072 | bytes 5898240 | tf_op jit(solution)/shard_map/pallas_call | solution.py:57
  (3 shorter events, 0.1 us)
Async XLA Ops:
  7.2 45.4 %all-gather.4.cloned.1.call-start = ((), (), s32[]{:S(2)}) async-start(), calls=%async_computation.3 | async-start | bytes 1966080 | tf_op jit(solution)/shard_map/all_gather | solution.py:133
  7.9 49.5 %collective-permute-start.1 = (bf16[384,512]{1,0:T(8,128)(2,1)}, bf16[384,512]{1,0:T(8,128)(2,1)S(1)}, u32[]{:S(2)}, u32[]{:S(2)}) collective-permute-start(bf16[384,512]{1,0:T(8,128)(2,1)} %bitcast.17), channel_id=1, source_target_pairs={{0,2},{1,0},{2,1},{3,5},{4,3},{5,4},{6,8},{7,6},{8,7},{9,11},{10,9... | collective-permute-start | bytes 1179656 | tf_op jit(solution)/shard_map/ppermute | solution.py:135
  23.0 34.3 %collective-permute-start = (bf16[384,512]{1,0:T(8,128)(2,1)}, bf16[384,512]{1,0:T(8,128)(2,1)S(1)}, u32[]{:S(2)}, u32[]{:S(2)}) collective-permute-start(bf16[384,512]{1,0:T(8,128)(2,1)} %bitcast.18), channel_id=1, source_target_pairs={{0,1},{1,2},{2,0},{3,4},{4,5},{5,3},{6,7},{7,8},{8,6},{9,10},{10,1... | collective-permute-start | bytes 1179656 | tf_op jit(solution)/shard_map/ppermute | solution.py:134
  27.6 33.3 %all-to-all-start = ((bf16[8,16,3584]{2,1,0:T(8,128)(2,1)}), bf16[8,16,3584]{2,1,0:T(8,128)(2,1)S(1)}, u32[]{:S(2)}, u32[]{:S(2)}) async-start(bf16[8,16,3584]{2,1,0:T(8,128)(2,1)} %copy.9), calls=%async_computation | async-start | bytes 1835008 | tf_op jit(solution)/shard_map/all_to_all | solution.py:142
  34.4 81.0 %all-gather.6.cloned.1.call-start = ((), (), s32[]{:S(2)}) async-start(), calls=%async_computation.4 | async-start | bytes 3932160 | tf_op jit(solution)/shard_map/all_gather | solution.py:148
  57.4 0.7 copy-start.4
  58.1 0.8 copy-start.5
  60.9 21.0 %copy-start.2 = (f32[16,448]{1,0:T(8,128)S(1)}, f32[16,448]{1,0:T(8,128)}, u32[]{:S(2)}) copy-start(f32[16,448]{1,0:T(8,128)} %param.8) | copy-start | bytes 86020
  60.9 21.0 %copy-start.3 = (f32[16,448]{1,0:T(8,128)S(1)}, f32[16,448]{1,0:T(8,128)}, u32[]{:S(2)}) copy-start(f32[16,448]{1,0:T(8,128)} %param.9) | copy-start | bytes 86020
  106.2 6.3 %copy-start = (bf16[32,16,448]{2,1,0:T(8,128)(2,1)}, bf16[32,16,448]{2,1,0:T(8,128)(2,1)S(1)}, u32[]{:S(2)}) copy-start(bf16[32,16,448]{2,1,0:T(8,128)(2,1)S(1)} %all_to_all.16.own_ref) | copy-start | bytes 1376260
  106.2 6.2 %collective-permute-start.2 = (bf16[32,16,448]{2,1,0:T(8,128)(2,1)S(1)}, bf16[32,16,448]{2,1,0:T(8,128)(2,1)S(1)}, u32[]{:S(2)}, u32[]{:S(2)}) collective-permute-start(bf16[32,16,448]{2,1,0:T(8,128)(2,1)S(1)} %all_to_all.16.own_ref), channel_id=1, source_target_pairs={{0,12},{12,0},{24,36},{36,24},{48,60},{60,48},{72,84},{84,72},{96,... | collective-permute-start | bytes 1376264 | tf_op jit(solution)/shard_map/ppermute | solution.py:114
  112.5 0.8 copy-start.1
Sparse Core Ops, SparseCore 0:
  10.4 42.1 all-gather.3
  61.0 50.5 all-gather.5

commit v3 on v2

--- a/solution.py
+++ b/solution.py
@@ -33,43 +33,8 @@
     return lax.all_to_all(copies, "replica", 0, 0, axis_index_groups=groups)
 
 
-def matmul_kernel(block_ref, token_ref, start_ref, *refs):
-    *weight_refs, out_ref = refs
-    total = start_ref[...].astype(jnp.float32)
-    index = 0
-    for weight_ref in weight_refs:
-        count, depth, _ = weight_ref.shape
-        for part in range(count):
-            columns = pl.ds(pl.multiple_of(block_ref[index] * 128, 128), depth)
-            total += jnp.dot(
-                token_ref[:, columns], weight_ref[part], preferred_element_type=jnp.float32
-            )
-            index += 1
-    out_ref[...] = total.astype(out_ref.dtype)
-
-
-def project(blocks, activation, weights, start, dtype, weigh=1):
-    tokens, features = activation.shape
-    width = weights[0].shape[-1]
-    tile = width // 2
-    out_spec = pl.BlockSpec((tokens, tile), lambda i, b: (0, i))
-    depth = sum(w.shape[0] * w.shape[1] for w in weights)
-    return pl.pallas_call(
-        matmul_kernel,
-        grid_spec=pltpu.PrefetchScalarGridSpec(
-            num_scalar_prefetch=1,
-            grid=(2,),
-            in_specs=[pl.BlockSpec((tokens, features), lambda i, b: (0, 0)), out_spec]
-            + [pl.BlockSpec(w.shape[:2] + (tile,), lambda i, b: (0, 0, i)) for w in weights],
-            out_specs=out_spec,
-        ),
-        out_shape=jax.ShapeDtypeStruct((tokens, width), dtype),
-        cost_estimate=pl.CostEstimate(
-            flops=2 * depth * tokens * width * weigh,
-            bytes_accessed=2 * depth * width + 2 * tokens * features + 6 * tokens * width,
-            transcendentals=0,
-        ),
-    )(blocks, activation, start, *weights)
+def dot(left, right):
+    return jnp.dot(left, right, preferred_element_type=jnp.float32)
 
 
 def update(summed, params, momentum):
@@ -79,24 +44,51 @@
     return new_params, new_momentum
 
 
-def pair_kernel(first_ref, second_ref, out_ref):
-    out_ref[0] = first_ref[...]
-    out_ref[1] = second_ref[...]
+def pass_kernel(first_ref, in_ref, out_ref):
+    out_ref[...] = in_ref[...]
 
 
-def pair(first, second):
-    rows, width = first.shape
-    part = pl.BlockSpec((rows // 2, width), lambda i: (i, 0))
+def passed_after(array, first):
+    whole = pl.BlockSpec(array.shape, lambda: (0, 0))
     return pl.pallas_call(
-        pair_kernel,
-        grid=(2,),
-        in_specs=[part, part],
-        out_specs=pl.BlockSpec((2, rows // 2, width), lambda i: (0, i, 0)),
-        out_shape=jax.ShapeDtypeStruct((2, rows, width), first.dtype),
+        pass_kernel,
+        in_specs=[pl.BlockSpec(memory_space=pl.ANY), whole],
+        out_specs=whole,
+        out_shape=jax.ShapeDtypeStruct(array.shape, array.dtype),
         cost_estimate=pl.CostEstimate(
-            flops=4 * 10**10, bytes_accessed=8 * rows * width, transcendentals=0
+            flops=4 * 10**10, bytes_accessed=8 * array.size, transcendentals=0
         ),
-    )(first, second)
+    )(first, array)
+
+
+def arrange_kernel(block_ref, near_in_ref, far_in_ref, near_ref, far_ref):
+    near_ref[...] = near_in_ref[...]
+    far_ref[...] = far_in_ref[...]
+
+
+def arrange(blocks, activation, depth):
+    tokens, _ = activation.shape
+    count = blocks.shape[0] - X
+    step = count // X
+
+    def columns(index):
+        return pl.BlockSpec((tokens, depth), index)
+
+    return pl.pallas_call(
+        arrange_kernel,
+        grid_spec=pltpu.PrefetchScalarGridSpec(
+            num_scalar_prefetch=1,
+            grid=(count,),
+            in_specs=[
+                columns(lambda i, b: (0, b[i // step])),
+                columns(lambda i, b: (0, b[X + i])),
+            ],
+            out_specs=[columns(lambda i, b: (0, i // step)), columns(lambda i, b: (0, i))],
+        ),
+        out_shape=[
+            jax.ShapeDtypeStruct((tokens, n * depth), activation.dtype) for n in (X, count)
+        ],
+    )(blocks, activation, activation)
 
 
 def assemble_kernel(core_ref, own_ref, other_ref, out_ref):
@@ -134,29 +126,32 @@
     from_below = lax.ppermute(weight, "fsdp", z_shift(1))
     from_above = lax.ppermute(weight, "fsdp", z_shift(-1))
     starts = jnp.arange(X, dtype=jnp.int32)[:, None] * ZH
-    zeros = jnp.zeros((activation.shape[0], weight.shape[1]), jnp.bfloat16)
-    near = (starts + z).astype(jnp.int32)
-    keys = project(near.ravel() * 3, activation, [own], zeros, jnp.float32)
+    near = starts + z
+    far = starts + jnp.stack([(z + 2) % ZH, (z + 1) % ZH])
+    blocks = jnp.concatenate([near.ravel(), far.ravel()]).astype(jnp.int32)
+    depth, width = weight.shape
+    near, far = arrange(blocks, activation, depth)
+    keys = dot(near, own.reshape(-1, width))
 
     parts = delta.reshape(rows, Y, columns // Y).transpose(1, 0, 2)
     parts = lax.all_to_all(parts, "replica", 0, 0, axis_index_groups=y_rings)
 
-    from_below, from_above, keys = lax.optimization_barrier((from_below, from_above, keys))
-    others = pair(from_below, from_above)
-    parts, others = lax.optimization_barrier((parts, others))
+    from_below, from_above, keys, far = lax.optimization_barrier(
+        (from_below, from_above, keys, far)
+    )
+    others = jnp.stack([from_below, from_above])
+    rest = lax.all_gather(others, "fsdp", axis=0, axis_index_groups=x_rings)
+    params = passed_after(params, others)
+    parts, params = lax.optimization_barrier((parts, params))
     summed = jnp.sum(parts.astype(jnp.float32), axis=0)
-    rest = lax.all_gather(others, "fsdp", axis=0, axis_index_groups=x_rings)
-
     parts = summed.reshape(rows, 8, columns // 64).transpose(1, 0, 2)
     parts = lax.all_to_all(parts, "replica", 0, 0, axis_index_groups=zc_groups)
     new_params, new_momentum = update(jnp.sum(parts, axis=0), params, momentum)
     merged = new_params.astype(jnp.bfloat16)
-
     merged_weights = assemble(spread(merged, same_core))
 
-    far = (starts + jnp.stack([(z + 2) % ZH, (z + 1) % ZH])).astype(jnp.int32)
-    rest = rest.reshape((-1,) + weight.shape)
-    keys = project(far.ravel() * 3, activation, [rest], keys, jnp.bfloat16)
+    keys += dot(far, rest.reshape(-1, width))
+    keys = keys.astype(jnp.bfloat16)
     return new_params, new_momentum, merged_weights, keys[None]
 
 

time: 128 us -> 125 us (0.977)
  matrix products: 0 us -> 4.89 us
  Pallas kernels: 13 us -> 10 us
  local copies, waits for them, and re-layouts: 6.56 us -> 3.88 us
  waiting for transfers between devices: 19 us -> 16.5 us
  other arithmetic: 1.47 us -> 3.28 us
  blocking collectives: 44.2 us -> 42.9 us
    ppermute x1, starting transfers between devices: 1.92 us -> 11.5 us  [local(): from_below = lax.ppermute(weight, 'fsdp', z_shift(1))]
    ppermute x1, starting transfers between devices: 15.1 us -> 5.56 us  [local(): from_above = lax.ppermute(weight, 'fsdp', z_shift(-1))]
    all_gather x1, waiting for transfers between devices: 17.6 us -> 10.6 us  [local(): own = lax.all_gather(weight, 'fsdp', axis=0, axis_index_groups=x_rings)]
    dot_general x0 -> x2, matrix products: none -> 4.89 us  [dot(): return jnp.dot(left, right, preferred_element_type=jnp.float32)]
    all_to_all x1, waiting for transfers between devices: 0.01 us -> 3.3 us  [local(): parts = lax.all_to_all(parts, 'replica', 0, 0, axis_index_groups=y_rings)]
    pallas_call x3 -> x2, Pallas kernels: 10.9 us -> 7.95 us  [the longest x1 6.57 us: arrange(): pl.pallas_call(arrange_kernel, grid_spec=pltpu.PrefetchScalarGridSpec(num...]
    unnamed x13 -> x11, local copies, waits for them, and re-layouts: 3.76 us -> 2.28 us
    all_to_all x1, blocking collectives: 20.5 us -> 19.1 us  [local(): parts = lax.all_to_all(parts, 'replica', 0, 0, axis_index_groups=zc_groups)]
  transfers between devices with their start and end apart: 6 -> 6, of which waited for: 2 -> 4; matrix products, arithmetic and copies ran while one was open for 5% -> 6% of each run, Pallas kernels for 6% -> 8%
where the time goes in v3:
time: 125 us; the launch traced here: 124 us
  blocking collectives  42.9 us (34%)
  starting transfers between devices  28.6 us (23%)
  waiting for transfers between devices  16.5 us (13%)
  between operations  14.2 us (11%)
  Pallas kernels  10 us (8%)
  matrix products  4.89 us (4%)
  local copies, waits for them, and re-layouts  3.88 us (3%)
  other arithmetic  3.28 us (3%)
    all_to_all x1, blocking collectives, spread(): return lax.all_to_all(copies, 'replica', 0, 0, axis_index_groups=groups)  23.8 us
    all_to_all x1, blocking collectives, local(): parts = lax.all_to_all(parts, 'replica', 0, 0, axis_index_groups=zc_groups)  19.1 us
    ppermute x1, starting transfers between devices, local(): from_below = lax.ppermute(weight, 'fsdp', z_shift(1))  11.5 us
    all_gather x1, waiting for transfers between devices, local(): own = lax.all_gather(weight, 'fsdp', axis=0, axis_index_groups=x_rings)  10.6 us
    all_to_all x1, starting transfers between devices, local(): parts = lax.all_to_all(parts, 'replica', 0, 0, axis_index_groups=y_rings)  6.82 us
    pallas_call x1, Pallas kernels, arrange(): pl.pallas_call(arrange_kernel, grid_spec=pltpu.PrefetchScalarGridSpec(num...  6.57 us
    ppermute x1, starting transfers between devices, local(): from_above = lax.ppermute(weight, 'fsdp', z_shift(-1))  5.56 us
    dot_general x2, matrix products, dot(): return jnp.dot(left, right, preferred_element_type=jnp.float32)  4.89 us
  transfers between devices with their start and end apart: 6, of which 4 were waited for; matrix products, arithmetic and copies ran while one was open for 6% of the time, Pallas kernels for 8%

profile of v3, /device:TPU:1, one launch (start us, length us, event | category | flops | bytes accessed | tf_op | source)
XLA Modules:
  0.0 124.4 jit_solution(5052940124935994707)
XLA Ops:
  7.2 0.0 all-gather.4.cloned.1.call-start
  7.2 0.7 all-gather.4.cloned.1.call-update
  7.9 11.5 %collective-permute-start = (bf16[384,512]{1,0:T(8,128)(2,1)}, bf16[384,512]{1,0:T(8,128)(2,1)S(1)}, u32[]{:S(2)}, u32[]{:S(2)}) collective-permute-start(bf16[384,512]{1,0:T(8,128)(2,1)} %bitcast.27), channel_id=1, source_target_pairs={{0,1},{1,2},{2,0},{3,4},{4,5},{5,3},{6,7},{7,8},{8,6},{9,10},{10,1... | collective-permute-start | bytes 1179656 | tf_op jit(solution)/shard_map/ppermute | solution.py:126
  19.4 5.6 %collective-permute-start.1 = (bf16[384,512]{1,0:T(8,128)(2,1)}, bf16[384,512]{1,0:T(8,128)(2,1)S(1)}, u32[]{:S(2)}, u32[]{:S(2)}) collective-permute-start(bf16[384,512]{1,0:T(8,128)(2,1)} %bitcast.28), channel_id=1, source_target_pairs={{0,2},{1,0},{2,1},{3,5},{4,3},{5,4},{6,8},{7,6},{8,7},{9,11},{10,9... | collective-permute-start | bytes 1179656 | tf_op jit(solution)/shard_map/ppermute | solution.py:127
  24.9 1.4 %copy.11 = bf16[2,8,8,3584]{3,2,1,0:T(8,128)(2,1)S(1)} copy(bf16[2,8,8,3584]{3,1,2,0:T(8,128)(2,1)} %bitcast.26) | data formatting | bytes 1835008
  26.4 1.2 copy.9
  27.6 6.8 %all-to-all-start = ((bf16[8,16,3584]{2,1,0:T(8,128)(2,1)}), bf16[8,16,3584]{2,1,0:T(8,128)(2,1)S(1)}, u32[]{:S(2)}, u32[]{:S(2)}) async-start(bf16[8,16,3584]{2,1,0:T(8,128)(2,1)} %copy.9), calls=%async_computation | async-start | bytes 1835008 | tf_op jit(solution)/shard_map/all_to_all | solution.py:137
  34.4 0.0 all-gather.6.cloned.1.call-start
  34.5 0.1 pad_add_fusion
  34.6 0.1 broadcast_add_fusion
  34.7 0.1 add.64
  34.8 0.6 pad_add_fusion.1.block_ref
  35.3 6.6 %shard_map.84 = (bf16[224,1536]{1,0:T(8,128)(2,1)}, bf16[224,3072]{1,0:T(8,128)(2,1)}) custom-call(s32[12]{0:T(128)} %pad_add_fusion.1.block_ref, bf16[224,4608]{1,0:T(8,128)(2,1)} %bitcast.21, bf16[224,4608]{1,0:T(8,128)(2,1)} %bitcast.22), custom_call_target="tpu_custom_call" | custom-call | tf_op jit(solution)/shard_map/pallas_call | solution.py:77
  41.9 10.6 %all-gather.4.cloned.1.call-done = bf16[4,384,512]{2,1,0:T(8,128)(2,1)} async-done(((bf16[1,384,512]{2,1,0:T(8,128)(2,1)}), bf16[4,384,512]{2,1,0:T(8,128)(2,1)}) %all-gather.4.cloned.1.call-update) | async-done | bytes 1572880 | tf_op jit(solution)/shard_map/all_gather | solution.py:125
  52.6 2.1 %fusion.2 = f32[224,512]{1,0:T(8,128)S(1)} fusion(bf16[224,1536]{1,0:T(8,128)(2,1)} %get-tuple-element.12, bf16[1536,512]{1,0:T(8,128)(2,1)} %bitcast.24), kind=kOutput, calls=%fused_computation.12 | convolution fusion | flops 352321536 | bytes 2719744 | tf_op jit(solution)/shard_map/dot_general | solution.py:37
  54.7 0.0 collective-permute-done
  54.7 0.4 collective-permute-done.1
  55.1 1.0 pad_maximum_fusion.first_ref
  56.1 0.0 all-gather.6.cloned.1.call-update
  56.1 1.4 %shard_map.85 = f32[16,448]{1,0:T(8,128)} custom-call(bf16[2,384,512]{2,1,0:T(8,128)(2,1)} %pad_maximum_fusion.first_ref, f32[16,448]{1,0:T(8,128)} %in_ref.1), custom_call_target="tpu_custom_call" | custom-call | flops 40000000000 | bytes 57344 | tf_op jit(solution)/shard_map/pallas_call | solution.py:53
  57.5 0.0 copy-start.2
  57.5 0.0 copy-start.3
  57.5 3.3 %all-to-all-done = bf16[8,16,3584]{2,1,0:T(8,128)(2,1)S(1)} async-done(((bf16[8,16,3584]{2,1,0:T(8,128)(2,1)}), bf16[8,16,3584]{2,1,0:T(8,128)(2,1)S(1)}, u32[]{:S(2)}, u32[]{:S(2)}) %all-to-all-start) | async-done | bytes 917536 | tf_op jit(solution)/shard_map/all_to_all | solution.py:137
  60.8 0.1 convert_reduce_fusion
  60.9 0.1 reshape.31
  61.1 0.2 copy.10
  61.2 19.1 %all_to_all.15 = f32[8,16,448]{2,1,0:T(8,128)S(1)} all-to-all(f32[8,16,448]{2,1,0:T(8,128)S(1)} %copy.10), channel_id=1, replica_groups={{0,12,24,36,48,60,72,84},{96,108,120,132,144,156,168,180},{192,204,216,..., dimensions={0} | all-to-all | bytes 458752 | tf_op jit(solution)/shard_map/all_to_all | solution.py:148
  80.4 0.0 copy-done.2
  80.4 0.0 copy-done.3
  80.4 0.6 fusion.1
  81.1 0.0 copy-start.4
  81.1 23.8 %all_to_all.16.own_ref = bf16[32,16,448]{2,1,0:T(8,128)(2,1)S(1)} all-to-all(bf16[32,16,448]{2,1,0:T(8,128)(2,1)S(1)} %broadcast_in_dim.12), channel_id=1, replica_groups={{0,24,48,72,96,120,144,168,192,216,240,264,288,312,336,360,384,408,432,..., dimensions={0} | all-to-all | bytes 917504 | tf_op jit(solution)/shard_map/all_to_all | solution.py:33
  104.9 0.0 copy-start
  104.9 4.7 %collective-permute-start.2 = (bf16[32,16,448]{2,1,0:T(8,128)(2,1)S(1)}, bf16[32,16,448]{2,1,0:T(8,128)(2,1)S(1)}, u32[]{:S(2)}, u32[]{:S(2)}) collective-permute-start(bf16[32,16,448]{2,1,0:T(8,128)(2,1)S(1)} %all_to_all.16.own_ref), channel_id=1, source_target_pairs={{0,12},{12,0},{24,36},{36,24},{48,60},{60,48},{72,84},{84,72},{96,... | collective-permute-start | bytes 1376264 | tf_op jit(solution)/shard_map/ppermute | solution.py:106
  109.6 1.5 %collective-permute-done.2.other_ref = bf16[32,16,448]{2,1,0:T(8,128)(2,1)S(1)} collective-permute-done((bf16[32,16,448]{2,1,0:T(8,128)(2,1)S(1)}, bf16[32,16,448]{2,1,0:T(8,128)(2,1)S(1)}, u32[]{:S(2)}, u32[]{:S(2)}) %collective-permute-start.2) | collective-permute-done | bytes 458784 | tf_op jit(solution)/shard_map/ppermute | solution.py:106
  111.1 0.0 copy-start.1
  111.1 0.0 copy-done
  111.1 0.8 copy-done.1
  111.9 2.1 %shard_map.86 = bf16[16,28672]{1,0:T(8,128)(2,1)} custom-call(s32[1]{0:T(128)} %bitcast.9.core_ref, bf16[32,16,448]{2,1,0:T(8,128)(2,1)} %copy-done, bf16[32,16,448]{2,1,0:T(8,128)(2,1)} %copy-done.1), custom_call_target="tpu_custom_call" | custom-call | tf_op jit(solution)/shard_map/pallas_call | solution.py:109
  114.0 0.0 all-gather.6.cloned.1.call-done
  114.0 0.0 copy-done.4
  114.0 2.8 %fusion.3 = f32[224,512]{1,0:T(8,128)S(1)} fusion(bf16[224,3072]{1,0:T(8,128)(2,1)S(1)} %copy-done.4, bf16[3072,512]{1,0:T(8,128)(2,1)} %bitcast.31), kind=kOutput, calls=%fused_computation.13 | convolution fusion | flops 704643072 | bytes 4980736 | tf_op jit(solution)/shard_map/dot_general | solution.py:37
  116.8 0.8 fusion
  (4 shorter events, 0.1 us)
Async XLA Ops:
  7.2 45.4 %all-gather.4.cloned.1.call-start = ((), (), s32[]{:S(2)}) async-start(), calls=%async_computation.3 | async-start | bytes 1966080 | tf_op jit(solution)/shard_map/all_gather | solution.py:125
  7.9 46.8 %collective-permute-start = (bf16[384,512]{1,0:T(8,128)(2,1)}, bf16[384,512]{1,0:T(8,128)(2,1)S(1)}, u32[]{:S(2)}, u32[]{:S(2)}) collective-permute-start(bf16[384,512]{1,0:T(8,128)(2,1)} %bitcast.27), channel_id=1, source_target_pairs={{0,1},{1,2},{2,0},{3,4},{4,5},{5,3},{6,7},{7,8},{8,6},{9,10},{10,1... | collective-permute-start | bytes 1179656 | tf_op jit(solution)/shard_map/ppermute | solution.py:126
  19.4 35.7 %collective-permute-start.1 = (bf16[384,512]{1,0:T(8,128)(2,1)}, bf16[384,512]{1,0:T(8,128)(2,1)S(1)}, u32[]{:S(2)}, u32[]{:S(2)}) collective-permute-start(bf16[384,512]{1,0:T(8,128)(2,1)} %bitcast.28), channel_id=1, source_target_pairs={{0,2},{1,0},{2,1},{3,5},{4,3},{5,4},{6,8},{7,6},{8,7},{9,11},{10,9... | collective-permute-start | bytes 1179656 | tf_op jit(solution)/shard_map/ppermute | solution.py:127
  27.6 33.2 %all-to-all-start = ((bf16[8,16,3584]{2,1,0:T(8,128)(2,1)}), bf16[8,16,3584]{2,1,0:T(8,128)(2,1)S(1)}, u32[]{:S(2)}, u32[]{:S(2)}) async-start(bf16[8,16,3584]{2,1,0:T(8,128)(2,1)} %copy.9), calls=%async_computation | async-start | bytes 1835008 | tf_op jit(solution)/shard_map/all_to_all | solution.py:137
  34.4 79.6 %all-gather.6.cloned.1.call-start = ((), (), s32[]{:S(2)}) async-start(), calls=%async_computation.4 | async-start | bytes 3932160 | tf_op jit(solution)/shard_map/all_gather | solution.py:143
  57.5 22.9 %copy-start.2 = (f32[16,448]{1,0:T(8,128)S(1)}, f32[16,448]{1,0:T(8,128)}, u32[]{:S(2)}) copy-start(f32[16,448]{1,0:T(8,128)} %param.9) | copy-start | bytes 86020
  57.5 22.9 %copy-start.3 = (f32[16,448]{1,0:T(8,128)S(1)}, f32[16,448]{1,0:T(8,128)}, u32[]{:S(2)}) copy-start(f32[16,448]{1,0:T(8,128)} %shard_map.85) | copy-start | bytes 86020
  81.1 33.0 %copy-start.4 = (bf16[224,3072]{1,0:T(8,128)(2,1)S(1)}, bf16[224,3072]{1,0:T(8,128)(2,1)}, u32[]{:S(2)}) copy-start(bf16[224,3072]{1,0:T(8,128)(2,1)} %get-tuple-element.19) | copy-start | bytes 4128772
  104.9 6.3 %copy-start = (bf16[32,16,448]{2,1,0:T(8,128)(2,1)}, bf16[32,16,448]{2,1,0:T(8,128)(2,1)S(1)}, u32[]{:S(2)}) copy-start(bf16[32,16,448]{2,1,0:T(8,128)(2,1)S(1)} %all_to_all.16.own_ref) | copy-start | bytes 1376260
  104.9 6.2 %collective-permute-start.2 = (bf16[32,16,448]{2,1,0:T(8,128)(2,1)S(1)}, bf16[32,16,448]{2,1,0:T(8,128)(2,1)S(1)}, u32[]{:S(2)}, u32[]{:S(2)}) collective-permute-start(bf16[32,16,448]{2,1,0:T(8,128)(2,1)S(1)} %all_to_all.16.own_ref), channel_id=1, source_target_pairs={{0,12},{12,0},{24,36},{36,24},{48,60},{60,48},{72,84},{84,72},{96,... | collective-permute-start | bytes 1376264 | tf_op jit(solution)/shard_map/ppermute | solution.py:106
  111.1 0.8 copy-start.1
Sparse Core Ops, SparseCore 0:
  10.4 42.1 all-gather.3
  56.2 53.8 all-gather.5
